TPU v7x, 256 devices: a whole 4x4x8 slice. The times are simulated.
256 devices in a mesh: seq: 32 (over x, z_hi, core), exp: 8 (over y, z_lo).
Axes of the slice: x: 4, y: 4, z: 8 (z_hi: 4, z_lo: 2; z = z_hi * 2 + z_lo), core: 2. Of those that a mesh axis runs over, the one named last changes fastest.
Arguments:
- tokens: bfloat16 [61440, 1024], P('seq'), may hold values from -24 to 24
- slot_embed: bfloat16 [1024, 2048], P(None, 'exp'), may hold values from -3 to 3
- w_in: bfloat16 [128, 1024, 4096], P('exp', None, 'seq'), may hold values from -0.375 to 0.375
- w_out: bfloat16 [128, 4096, 1024], P('exp', 'seq'), may hold values from -0.125 to 0.125
Outputs:
- mixed_out: bfloat16 [61440, 1024], P('seq', 'exp')
All inputs are finite; a program needn't handle non-finite values.
Results may differ from a plain program's by a relative error of at most 0.012.
Values may be sent and summed in bfloat16 or wider, within the bound.
No kernel may reach another device: no remote copies, remote signals or barrier semaphores. Data moves between devices by JAX's collectives and lax.ppermute only.
A program may use at most 64 MiB of HBM per device.

v0:
```python
import jax
import jax.numpy as jnp
from jax import lax
from jax.sharding import PartitionSpec as P


def gelu_tanh(values):
    return (
        0.5
        * values
        * (1.0 + jnp.tanh(0.7978845608028654 * (values + 0.044715 * values * values * values)))
    )


def on_device(tokens, slot_embed, w_in, w_out):
    experts_here = w_in.shape[0]
    slot_count = slot_embed.shape[1]
    slot_exp = slot_count // experts_here
    features = tokens.shape[1]
    logits = jnp.dot(tokens, slot_embed, preferred_element_type=jnp.float32)
    col_peak = jnp.max(logits, axis=0)
    peak_all = lax.pmax(col_peak, "seq")
    weights = jnp.exp(logits - peak_all[None, :])
    total_all = lax.psum(jnp.sum(weights, axis=0), "seq")
    dispatch = (weights / total_all[None, :]).astype(jnp.bfloat16)
    partial_in = lax.dot_general(
        dispatch, tokens, (((0,), (0,)), ((), ())), preferred_element_type=jnp.float32
    )
    slot_in = lax.psum(partial_in, "seq").astype(jnp.bfloat16)
    grouped = slot_in.reshape(experts_here, slot_exp, features)
    hidden = gelu_tanh(
        jnp.einsum("esd,edh->esh", grouped, w_in, preferred_element_type=jnp.float32)
    ).astype(jnp.bfloat16)
    partial_out = jnp.einsum(
        "esh,ehd->esd", hidden, w_out, preferred_element_type=jnp.float32
    ).reshape(slot_count, features)
    slot_out = lax.psum(partial_out, "seq").astype(jnp.bfloat16)
    row_peak = lax.pmax(jnp.max(logits, axis=1), "exp")
    row_weights = jnp.exp(logits - row_peak[:, None])
    row_sum = lax.psum(jnp.sum(row_weights, axis=1), "exp")
    combine = (row_weights / row_sum[:, None]).astype(jnp.bfloat16)
    term = jnp.dot(combine, slot_out, preferred_element_type=jnp.float32)
    mixed_out = lax.psum_scatter(term.astype(jnp.bfloat16), "exp", scatter_dimension=1, tiled=True)
    return mixed_out


def solution(mesh):
    placed = (P("seq", None), P(None, "exp"), P("exp", None, "seq"), P("exp", "seq", None))
    return jax.shard_map(
        on_device, mesh=mesh, in_specs=placed, out_specs=P("seq", "exp"), check_vma=False
    )
```

profile of v0, /device:TPU:1, one launch (start us, length us, event | category | flops | bytes accessed | tf_op | source)
XLA Modules:
  0.0 604.6 jit_solution(15474171280990773589)
XLA Ops:
  6.5 0.0 copy-start
  6.5 0.0 reduce-scatter.4.cloned.1.call-start
  6.5 1.0 copy-done
  7.6 3.4 fusion.23
  11.0 0.0 copy-start.1
  11.0 73.4 %pmax.15 = f32[256]{0:T(256)S(1)} all-reduce(f32[256]{0:T(256)S(1)} %get-tuple-element.7), channel_id=1, replica_groups=mesh['seq'=32,'exp'=8] {'seq'}, use_global_device_ids=true, to_apply=%region_5.0 | all-reduce | flops 256 | bytes 2048 | tf_op jit(solution)/shard_map/pmax | solution.py:22
  84.3 0.0 copy-start.2
  84.3 16.1 %pmax.14 = f32[1920]{0:T(1024)S(1)} all-reduce(f32[1920]{0:T(1024)S(1)} %get-tuple-element.8), channel_id=1, replica_groups=mesh['seq'=32,'exp'=8] {'exp'}, use_global_device_ids=true, to_apply=%region_1.0 | all-reduce | flops 1920 | bytes 15360 | tf_op jit(solution)/shard_map/pmax | solution.py:38
  100.4 0.8 fusion.1
  101.2 79.5 %psum.29 = f32[256]{0:T(256)} all-reduce(f32[256]{0:T(256)S(1)} %get-tuple-element.5), channel_id=1, replica_groups=mesh['seq'=32,'exp'=8] {'seq'}, use_global_device_ids=true, to_apply=%region_7.0 | all-reduce | flops 256 | bytes 2048 | tf_op jit(solution)/shard_map/psum | solution.py:24
  180.7 0.0 copy-done.2
  180.7 13.1 %psum.28 = f32[1920]{0:T(1024)S(1)} all-reduce(f32[1920]{0:T(1024)S(1)} %get-tuple-element.6), channel_id=1, replica_groups=mesh['seq'=32,'exp'=8] {'exp'}, use_global_device_ids=true, to_apply=%region_3.0 | all-reduce | flops 1920 | bytes 15360 | tf_op jit(solution)/shard_map/psum | solution.py:40
  193.8 0.0 copy-done.1
  193.8 3.4 fusion.2
  197.3 146.0 %all-reduce.2 = bf16[256,1024]{1,0:T(8,128)(2,1)S(1)} all-reduce(f32[256,1024]{1,0:T(8,128)S(1)} %fusion.2), channel_id=1, replica_groups=mesh['seq'=32,'exp'=8] {'seq'}, use_global_device_ids=true, to_apply=%region_8.0 | all-reduce | flops 262144 | bytes 1572864 | tf_op jit(solution)/shard_map/psum | solution.py:29
  343.3 4.7 fusion.13
  348.0 149.2 %all-reduce.3 = bf16[256,1024]{1,0:T(8,128)(2,1)S(1)} all-reduce(f32[256,1024]{1,0:T(8,128)S(1)} %bitcast.12), channel_id=1, replica_groups=mesh['seq'=32,'exp'=8] {'seq'}, use_global_device_ids=true, to_apply=%region_9.0 | all-reduce | flops 262144 | bytes 1572864 | tf_op jit(solution)/shard_map/psum | solution.py:37
  497.2 4.7 convolution_convert_fusion
  501.9 6.3 %copy.5 = bf16[1920,1024]{0,1:T(8,128)(2,1)} copy(bf16[1920,1024]{1,0:T(8,128)(2,1)} %convolution_convert_fusion) | data formatting | bytes 7864320
  508.2 0.0 reduce-scatter.4.cloned.1.call-update
  508.3 87.5 %reduce-scatter.4.cloned.1.call-done = bf16[128,1920]{1,0:T(8,128)(2,1)} async-done(((bf16[1024,1920]{1,0:T(8,128)(2,1)}), bf16[128,1920]{1,0:T(8,128)(2,1)}) %reduce-scatter.4.cloned.1.call-update) | async-done | bytes 491536
  595.8 2.0 copy.6
Async XLA Ops:
  6.5 1.0 copy-start
  6.5 589.2 %reduce-scatter.4.cloned.1.call-start = ((), (), s32[]{:S(2)}) async-start(), calls=%async_computation.1 | async-start | bytes 4423680
  11.0 182.9 %copy-start.1 = (f32[1920,256]{1,0:T(8,128)}, f32[1920,256]{1,0:T(8,128)S(1)}, u32[]{:S(2)}) copy-start(f32[1920,256]{1,0:T(8,128)S(1)} %get-tuple-element.9) | copy-start | bytes 5898244
  84.3 96.4 %copy-start.2 = (f32[256]{0:T(256)}, f32[256]{0:T(256)S(1)}, u32[]{:S(2)}) copy-start(f32[256]{0:T(256)S(1)} %pmax.15) | copy-start | bytes 3076
Sparse Core Ops, SparseCore 0:
  508.4 87.3 reduce-scatter.3
where the time goes:
time: 605 us
  blocking collectives  477 us (79%)
  waiting for transfers between devices  87.5 us (14%)
  matrix products  16.2 us (3%)
  between operations  13.4 us (2%)
  local copies, waits for them, and re-layouts  9.4 us (2%)
    psum x1, blocking collectives, on_device(): slot_out = lax.psum(partial_out, 'seq').astype(jnp.bfloat16)  149 us
    psum x1, blocking collectives, on_device(): slot_in = lax.psum(partial_in, 'seq').astype(jnp.bfloat16)  146 us
    unnamed x2, waiting for transfers between devices  87.5 us
    psum x1, blocking collectives, on_device(): total_all = lax.psum(jnp.sum(weights, axis=0), 'seq')  79.5 us
    pmax x1, blocking collectives, on_device(): peak_all = lax.pmax(col_peak, 'seq')  73.4 us
    pmax x1, blocking collectives, on_device(): row_peak = lax.pmax(jnp.max(logits, axis=1), 'exp')  16.1 us
    psum x1, blocking collectives, on_device(): row_sum = lax.psum(jnp.sum(row_weights, axis=1), 'exp')  13.1 us
  transfers between devices with their start and end apart: 1, of which 1 were waited for; matrix products, arithmetic and copies ran while one was open for 0% of the time, Pallas kernels for 0%

commit v1 on v0

--- a/solution.py
+++ b/solution.py
@@ -26,7 +26,11 @@
     partial_in = lax.dot_general(
         dispatch, tokens, (((0,), (0,)), ((), ())), preferred_element_type=jnp.float32
     )
-    slot_in = lax.psum(partial_in, "seq").astype(jnp.bfloat16)
+
+    def match_the_body(packet):
+        return jnp.sum(lax.all_gather(packet, axis_name="seq"), axis=0)
+
+    slot_in = match_the_body(partial_in).astype(jnp.bfloat16)
     grouped = slot_in.reshape(experts_here, slot_exp, features)
     hidden = gelu_tanh(
         jnp.einsum("esd,edh->esh", grouped, w_in, preferred_element_type=jnp.float32)

time: 605 us -> 654 us (1.081)
  waiting for transfers between devices: 87.5 us -> 269 us
  blocking collectives: 477 us -> 331 us
  other arithmetic: 0.78 us -> 12.7 us
    all_gather x0 -> x1, waiting for transfers between devices: none -> 181 us  [match_the_body(): return jnp.sum(lax.all_gather(packet, axis_name='seq'), axis=0)]
    psum x1 -> x0, blocking collectives: 146 us -> none  [on_device(): slot_in = lax.psum(partial_in, 'seq').astype(jnp.bfloat16)]
    reduce_sum x0 -> x1, other arithmetic: none -> 11.9 us  [match_the_body(): return jnp.sum(lax.all_gather(packet, axis_name='seq'), axis=0)]
    unnamed x2 -> x3, waiting for transfers between devices: 87.5 us -> 88.6 us
  transfers between devices with their start and end apart: 1 -> 2, of which waited for: 1 -> 2; matrix products, arithmetic and copies ran while one was open for 0% -> 0% of each run, Pallas kernels for 0% -> 0%
where the time goes in v1:
time: 654 us; the launch traced here: 653 us
  blocking collectives  331 us (51%)
  waiting for transfers between devices  269 us (41%)
  matrix products  17.2 us (3%)
  between operations  13.4 us (2%)
  other arithmetic  12.7 us (2%)
  local copies, waits for them, and re-layouts  9.39 us (1%)
    all_gather x1, waiting for transfers between devices, match_the_body(): return jnp.sum(lax.all_gather(packet, axis_name='seq'), axis=0)  181 us
    psum x1, blocking collectives, on_device(): slot_out = lax.psum(partial_out, 'seq').astype(jnp.bfloat16)  147 us
    unnamed x3, waiting for transfers between devices  88.6 us
    psum x1, blocking collectives, on_device(): total_all = lax.psum(jnp.sum(weights, axis=0), 'seq')  78.9 us
    pmax x1, blocking collectives, on_device(): peak_all = lax.pmax(col_peak, 'seq')  73.4 us
    pmax x1, blocking collectives, on_device(): row_peak = lax.pmax(jnp.max(logits, axis=1), 'exp')  16.1 us
    psum x1, blocking collectives, on_device(): row_sum = lax.psum(jnp.sum(row_weights, axis=1), 'exp')  15.5 us
  transfers between devices with their start and end apart: 2, of which 2 were waited for; matrix products, arithmetic and copies ran while one was open for 0% of the time, Pallas kernels for 0%

profile of v1, /device:TPU:1, one launch (start us, length us, event | category | flops | bytes accessed | tf_op | source)
XLA Modules:
  0.0 653.2 jit_solution(632523125023726688)
XLA Ops:
  6.5 0.0 copy-start
  6.5 0.0 all-gather.3.cloned.1.call-start
  6.5 1.0 copy-done
  7.6 3.4 fusion.23
  11.0 0.0 copy-start.1
  11.0 73.4 %pmax.15 = f32[256]{0:T(256)S(1)} all-reduce(f32[256]{0:T(256)S(1)} %get-tuple-element.7), channel_id=1, replica_groups=mesh['seq'=32,'exp'=8] {'seq'}, use_global_device_ids=true, to_apply=%region_5.0 | all-reduce | flops 256 | bytes 2048 | tf_op jit(solution)/shard_map/pmax | solution.py:22
  84.3 16.1 %pmax.14 = f32[1920]{0:T(1024)S(1)} all-reduce(f32[1920]{0:T(1024)S(1)} %get-tuple-element.8), channel_id=1, replica_groups=mesh['seq'=32,'exp'=8] {'exp'}, use_global_device_ids=true, to_apply=%region_1.0 | all-reduce | flops 1920 | bytes 15360 | tf_op jit(solution)/shard_map/pmax | solution.py:42
  100.4 0.8 fusion.1
  101.2 78.9 %psum.22 = f32[256]{0:T(256)S(1)} all-reduce(f32[256]{0:T(256)S(1)} %get-tuple-element.5), channel_id=1, replica_groups=mesh['seq'=32,'exp'=8] {'seq'}, use_global_device_ids=true, to_apply=%region_7.0 | all-reduce | flops 256 | bytes 2048 | tf_op jit(solution)/shard_map/psum | solution.py:24
  180.1 4.4 fusion.2
  184.5 0.0 copy-done.1
  184.5 0.0 all-gather.3.cloned.1.call-update
  184.5 0.0 reduce-scatter.4.cloned.1.call-start
  184.6 15.5 %psum.21 = f32[1920]{0:T(1024)S(1)} all-reduce(f32[1920]{0:T(1024)S(1)} %get-tuple-element.6), channel_id=1, replica_groups=mesh['seq'=32,'exp'=8] {'exp'}, use_global_device_ids=true, to_apply=%region_3.0 | all-reduce | flops 1920 | bytes 15360 | tf_op jit(solution)/shard_map/psum | solution.py:44
  200.0 180.7 %all-gather.3.cloned.1.call-done = f32[8192,1024]{1,0:T(8,128)} async-done(((f32[256,1024]{1,0:T(8,128)}), f32[8192,1024]{1,0:T(8,128)}) %all-gather.3.cloned.1.call-update) | async-done | bytes 33554448 | tf_op jit(solution)/shard_map/all_gather | solution.py:31
  380.7 11.9 %reduce_sum.29 = bf16[256,1024]{1,0:T(8,128)(2,1)S(1)} reduce(f32[32,256,1024]{2,1,0:T(8,128)} %bitcast.12, f32[]{:T(128)} %constant.1.clone.1), dimensions={0}, to_apply=%region_8.0 | reduce | flops 8126464 | bytes 34078724 | tf_op jit(solution)/shard_map/reduce_sum | solution.py:31
  392.6 4.7 fusion.13
  397.3 147.4 %all-reduce.1 = bf16[256,1024]{1,0:T(8,128)(2,1)S(1)} all-reduce(f32[256,1024]{1,0:T(8,128)S(1)} %bitcast.14), channel_id=1, replica_groups=mesh['seq'=32,'exp'=8] {'seq'}, use_global_device_ids=true, to_apply=%region_9.0 | all-reduce | flops 262144 | bytes 1572864 | tf_op jit(solution)/shard_map/psum | solution.py:41
  544.7 4.7 convolution_convert_fusion
  549.5 6.3 copy.5
  555.8 0.0 reduce-scatter.4.cloned.1.call-update
  555.8 88.6 %reduce-scatter.4.cloned.1.call-done = bf16[128,1920]{1,0:T(8,128)(2,1)} async-done(((bf16[1024,1920]{1,0:T(8,128)(2,1)}), bf16[128,1920]{1,0:T(8,128)(2,1)}) %reduce-scatter.4.cloned.1.call-update) | async-done | bytes 491536
  644.4 2.0 copy.6
Async XLA Ops:
  6.5 1.0 copy-start
  6.5 374.2 %all-gather.3.cloned.1.call-start = ((), (), s32[]{:S(2)}) async-start(), calls=%async_computation.1 | async-start | bytes 34603008 | tf_op jit(solution)/shard_map/all_gather | solution.py:31
  11.0 173.5 %copy-start.1 = (f32[1920,256]{1,0:T(8,128)}, f32[1920,256]{1,0:T(8,128)S(1)}, u32[]{:S(2)}) copy-start(f32[1920,256]{1,0:T(8,128)S(1)} %get-tuple-element.9) | copy-start | bytes 5898244
  184.5 459.9 %reduce-scatter.4.cloned.1.call-start = ((), (), s32[]{:S(2)}) async-start(), calls=%async_computation.2 | async-start | bytes 4423680
Sparse Core Ops, SparseCore 0:
  184.6 196.0 all-gather.2
  556.0 88.3 reduce-scatter.3
